TPU v7x, 32 devices: a whole 2x2x4 slice. The times are simulated.
32 devices in a mesh: wide: 16 (over z, y, x), narrow: 2 (over core).
Axes of the slice: x: 2, y: 2, z: 4, core: 2. Of those that a mesh axis runs over, the one named last changes fastest.
Arguments:
- amplitudes: bfloat16 [384, 512], P('wide', 'narrow'), may hold values from -6 to 6
- integrals: bfloat16 [262144, 512], P('wide', 'narrow'), may hold values from -0.75 to 0.75
- virtual_irrep: int32 [512], replicated, may hold values from 0 to 7
- column_irrep: int32 [512], P('narrow'), may hold values from 0 to 7
- pair_energy: float32 [384], P('narrow'), may hold values from -4 to -1
- virtual_energy: float32 [512], replicated, may hold values from 0.5 to 3
- residual_in: bfloat16 [384, 262144], P('narrow', 'wide'), may hold values from -6 to 6
Outputs:
- new_amplitudes: bfloat16 [384, 262144], P('narrow', 'wide')
All inputs are finite; a program needn't handle non-finite values.
Results may differ from a plain program's by a relative error of at most 0.012.
Values may be sent and summed in bfloat16 or wider, within the bound.
A program may use at most 128 MiB of HBM per device.

v0:
```python
import jax
import jax.numpy as jnp
from jax import lax
from jax.sharding import PartitionSpec as P


def local(
    amplitudes, integrals, virtual_irrep, column_irrep, pair_energy, virtual_energy, residual_in
):
    wide_size = lax.axis_size("wide")
    num_virt = virtual_irrep.shape[0]
    a_local = num_virt // wide_size
    first_a = lax.axis_index("wide") * a_local
    local_irrep = lax.dynamic_slice_in_dim(virtual_irrep, first_a, a_local, 0)
    row_irrep = jnp.bitwise_xor(local_irrep[:, None], virtual_irrep[None, :]).reshape(
        a_local * num_virt
    )
    masked = jnp.where(
        row_irrep[:, None] == column_irrep[None, :], integrals, jnp.zeros((), integrals.dtype)
    )
    contract = (((1,), (1,)), ((), ()))
    terms = lax.dot_general(
        lax.all_gather(amplitudes, "wide", axis=0, tiled=True),
        masked,
        contract,
        preferred_element_type=jnp.float32,
    )
    ladder = lax.psum_scatter(
        terms.astype(jnp.bfloat16), "narrow", scatter_dimension=0, tiled=True
    ).astype(jnp.float32)
    pair_rows = ladder.shape[0]
    ladder_cube = ladder.reshape(pair_rows, a_local, num_virt)
    swapped = lax.all_to_all(
        ladder_cube.astype(jnp.bfloat16), "wide", split_axis=2, concat_axis=2, tiled=True
    ).astype(ladder_cube.dtype)
    mirrored = swapped.reshape(pair_rows, a_local, wide_size, a_local)
    mirrored = jnp.transpose(mirrored, (0, 3, 2, 1)).reshape(pair_rows, a_local * num_virt)
    local_energy = lax.dynamic_slice_in_dim(virtual_energy, first_a, a_local, 0)
    denominator = (
        pair_energy[:, None, None] - local_energy[None, :, None] - virtual_energy[None, None, :]
    )
    denominator = denominator.reshape(pair_rows, a_local * num_virt)
    total = residual_in.astype(jnp.float32) + ladder - mirrored
    return (total / denominator).astype(jnp.bfloat16)


def solution(mesh):
    return jax.shard_map(
        local,
        mesh=mesh,
        in_specs=(
            P("wide", "narrow"),
            P("wide", "narrow"),
            P(),
            P("narrow"),
            P("narrow"),
            P(),
            P("narrow", "wide"),
        ),
        out_specs=P("narrow", "wide"),
        check_vma=False,
    )
```

profile of v0, /device:TPU:28, one launch (start us, length us, event | category | flops | bytes accessed | tf_op | source)
XLA Modules:
  0.0 357.6 jit_solution(9107963849591281468)
XLA Ops:
  6.5 0.0 reduce-scatter.4.cloned.1.call-start
  6.5 35.6 %all_gather.3 = bf16[384,256]{1,0:T(8,128)(2,1)S(1)} all-gather(bf16[24,256]{1,0:T(8,128)(2,1)} %param.7), channel_id=1, replica_groups=mesh['wide'=16,'narrow'=2] {'wide'}, dimensions={0}, use_global_device_ids=true | all-gather | bytes 208896 | tf_op jit(solution)/shard_map/all_gather | solution.py:23
  42.2 0.8 dynamic_slice.6
  42.9 0.8 xor_bitcast_fusion
  43.7 10.4 %fusion = bf16[384,16384]{0,1:T(8,128)(2,1)} fusion(bf16[384,256]{1,0:T(8,128)(2,1)S(1)} %all_gather.3, bf16[16384,256]{1,0:T(8,128)(2,1)} %param.8, s32[256]{0:T(256)} %param.10, s32[16384]{0:T(1024)S(1)} %bitcast.27), kind=kOutput, calls=%fused_computation.1 | convolution fusion | flops 3235905536 | bytes 21234688 | tf_op jit(solution)/shard_map/dot_general | solution.py:22
  54.1 16.7 %copy.15 = bf16[384,16384]{1,0:T(8,128)(2,1)} copy(bf16[384,16384]{0,1:T(8,128)(2,1)} %fusion) | data formatting | bytes 25165824
  70.8 0.0 reduce-scatter.4.cloned.1.call-update
  70.8 24.0 %reduce-scatter.4.cloned.1.call-done = bf16[192,16384]{1,0:T(8,128)(2,1)} async-done(((bf16[384,16384]{1,0:T(8,128)(2,1)}), bf16[192,16384]{1,0:T(8,128)(2,1)}) %reduce-scatter.4.cloned.1.call-update) | async-done | bytes 6291472
  94.8 10.0 %copy.16 = bf16[192,16384]{0,1:T(8,128)(2,1)} copy(bf16[192,16384]{1,0:T(8,128)(2,1)} %reduce-scatter.4.cloned.1.call-done) | data formatting | bytes 12582912
  104.8 11.4 %copy.12 = bf16[192,32,512]{0,1,2:T(8,128)(2,1)} copy(bf16[192,32,512]{0,2,1:T(8,128)(2,1)} %bitcast.25) | data formatting | bytes 12582912 | tf_op jit(solution)/shard_map/convert_element_type | solution.py:34
  116.2 6.9 %all-to-all-start = ((bf16[192,32,512]{0,1,2:T(8,128)(2,1)}), bf16[192,32,512]{0,1,2:T(8,128)(2,1)}, u32[]{:S(2)}, u32[]{:S(2)}) async-start(bf16[192,32,512]{0,1,2:T(8,128)(2,1)} %copy.12), calls=%async_computation | async-start | bytes 16777216 | tf_op jit(solution)/shard_map/all_to_all | solution.py:33
  123.1 0.0 copy-start
  123.1 0.0 copy-start.1
  123.1 10.0 %copy.11 = bf16[192,16384]{0,1:T(8,128)(2,1)} copy(bf16[192,16384]{1,0:T(8,128)(2,1)} %param.13) | data formatting | bytes 12582912 | tf_op args[6]
  133.1 0.0 copy-done
  133.1 0.1 dynamic_slice.7
  133.2 0.0 copy-done.1
  133.2 0.1 broadcast_subtract_fusion
  133.3 180.9 %all-to-all-done = bf16[192,32,512]{0,1,2:T(8,128)(2,1)} async-done(((bf16[192,32,512]{0,1,2:T(8,128)(2,1)}), bf16[192,32,512]{0,1,2:T(8,128)(2,1)}, u32[]{:S(2)}, u32[]{:S(2)}) %all-to-all-start) | async-done | bytes 6291488 | tf_op jit(solution)/shard_map/all_to_all | solution.py:33
  314.2 11.3 %copy.13 = f32[192,32,16,32]{0,1,2,3:T(8,128)} copy(bf16[192,32,16,32]{0,1,3,2:T(8,128)(2,1)} %bitcast.7) | data formatting | bytes 18874368 | tf_op jit(solution)/shard_map/reshape | solution.py:37
  325.5 15.1 %fusion.2 = bf16[192,16384]{0,1:T(8,128)(2,1)} fusion(f32[192,32,16,32]{0,1,2,3:T(8,128)} %copy.13, bf16[192,16384]{0,1:T(8,128)(2,1)} %copy.16, bf16[192,16384]{0,1:T(8,128)(2,1)} %copy.11, f32[16384]{0:T(1024)S(1)} %bitcast.26, f32[192,32]{0,1:T(8,128)S(1)} %broadcast_subtract_fusion), kind=kLoop, calls=%fused_computation.4 | loop fusion | flops 22020096 | bytes 31547392 | tf_op jit(solution)/shard_map/convert_element_type | solution.py:44
  340.6 10.1 %copy.14 = bf16[192,16384]{1,0:T(8,128)(2,1)} copy(bf16[192,16384]{0,1:T(8,128)(2,1)} %fusion.2) | data formatting | bytes 12582912 | tf_op jit(solution)/shard_map/convert_element_type | solution.py:44
  (3 shorter events, 0.0 us)
Async XLA Ops:
  6.5 88.3 %reduce-scatter.4.cloned.1.call-start = ((), (), s32[]{:S(2)}) async-start(), calls=%async_computation.2 | async-start | bytes 18874368
  116.2 198.0 %all-to-all-start = ((bf16[192,32,512]{0,1,2:T(8,128)(2,1)}), bf16[192,32,512]{0,1,2:T(8,128)(2,1)}, u32[]{:S(2)}, u32[]{:S(2)}) async-start(bf16[192,32,512]{0,1,2:T(8,128)(2,1)} %copy.12), calls=%async_computation | async-start | bytes 16777216 | tf_op jit(solution)/shard_map/all_to_all | solution.py:33
  123.1 10.0 %copy-start = (f32[512]{0:T(512)S(1)}, f32[512]{0:T(512)}, u32[]{:S(2)}) copy-start(f32[512]{0:T(512)} %param.12) | copy-start | bytes 6148
  123.1 10.1 %copy-start.1 = (f32[192]{0:T(256)S(1)}, f32[192]{0:T(256)}, u32[]{:S(2)}) copy-start(f32[192]{0:T(256)} %param.11) | copy-start | bytes 2308
Sparse Core Ops, SparseCore 0:
  70.9 23.8 reduce-scatter.3
where the time goes:
time: 359 us; the launch traced here: 358 us
  waiting for transfers between devices  205 us (57%)
  local copies, waits for them, and re-layouts  70.3 us (20%)
  blocking collectives  35.6 us (10%)
  other arithmetic  15.9 us (4%)
  between operations  13.4 us (4%)
  matrix products  10.4 us (3%)
  starting transfers between devices  6.92 us (2%)
    all_to_all x1, waiting for transfers between devices, local(): lax.all_to_all(ladder_cube.astype(jnp.bfloat16), 'wide', split_axis=2, co...  181 us
    unnamed x10, local copies, waits for them, and re-layouts  36.7 us
    all_gather x1, blocking collectives, local(): lax.all_gather(amplitudes, 'wide', axis=0, tiled=True)  35.6 us
    unnamed x2, waiting for transfers between devices  24 us
    convert_element_type x1, other arithmetic, local(): return (total / denominator).astype(jnp.bfloat16)  15.1 us
    convert_element_type x1, local copies, waits for them, and re-layouts, local(): ladder_cube.astype(jnp.bfloat16)  11.4 us
    reshape x1, local copies, waits for them, and re-layouts, local(): jnp.transpose(mirrored, (0, 3, 2, 1)).reshape(pair_rows, a_local * num_virt)  11.3 us
    dot_general x1, matrix products, local(): lax.dot_general(lax.all_gather(amplitudes, 'wide', axis=0, tiled=True), m...  10.4 us
  transfers between devices with their start and end apart: 2, of which 2 were waited for; matrix products, arithmetic and copies ran while one was open for 3% of the time, Pallas kernels for 0%

commit v1 on v0

--- a/solution.py
+++ b/solution.py
@@ -1,10 +1,19 @@
+import functools
+
 import jax
 import jax.numpy as jnp
 from jax import lax
+from jax.experimental import pallas as pl
+from jax.experimental.pallas import tpu as pltpu
 from jax.sharding import PartitionSpec as P
 
-
-def local(
+SLOTS = 64
+MESH = pl.DeviceIdType.MESH
+BF16 = jnp.bfloat16
+F32 = jnp.float32
+
+
+def dense(
     amplitudes, integrals, virtual_irrep, column_irrep, pair_energy, virtual_energy, residual_in
 ):
     wide_size = lax.axis_size("wide")
@@ -44,9 +53,275 @@
     return (total / denominator).astype(jnp.bfloat16)
 
 
+def partner(me, step, n):
+    result, bit = 0, 1
+    while bit < n:
+        result += ((me // bit + step // bit) % 2) * bit
+        bit *= 2
+    return result
+
+
+def exchange_kernel(
+    n, v_ref, irb_ref, colx_ref, s_ref, lc_ref, rx_ref,
+    vbuf, fbuf, tx, lcbuf, load_sem, send_sem, recv_sem, fsend_sem, frecv_sem, own_sem, lc_sem,
+):
+    me, core = lax.axis_index("wide"), lax.axis_index("narrow")
+    other = 1 - core
+    al = v_ref.shape[0]
+    half = al // 2
+    width = v_ref.shape[2]
+
+    def load(i):
+        to = partner(me, n - 1 - i, n)
+        columns = pl.ds(pl.multiple_of(to * al, al), al)
+        return pltpu.make_async_copy(v_ref.at[:, columns, :], vbuf.at[i], load_sem.at[i])
+
+    def send(i):
+        to = partner(me, n - 1 - i, n)
+        return pltpu.make_async_remote_copy(
+            src_ref=tx.at[i], dst_ref=rx_ref.at[core, me], send_sem=send_sem.at[i],
+            recv_sem=recv_sem.at[i], device_id=(to, core), device_id_type=MESH,
+        )
+
+    def arrival(i):
+        source = partner(me, n - 1 - i, n)
+        return pltpu.make_async_remote_copy(
+            src_ref=tx.at[i], dst_ref=rx_ref.at[core, source], send_sem=send_sem.at[i],
+            recv_sem=recv_sem.at[i], device_id=(source, core), device_id_type=MESH,
+        )
+
+    def forward(i):
+        source = partner(me, n - 1 - i, n)
+        return pltpu.make_async_remote_copy(
+            src_ref=rx_ref.at[core, source], dst_ref=rx_ref.at[core, source],
+            send_sem=fsend_sem.at[i], recv_sem=frecv_sem.at[i],
+            device_id=(me, other), device_id_type=MESH,
+        )
+
+    def forwarded(i):
+        source = partner(me, n - 1 - i, n)
+        return pltpu.make_async_remote_copy(
+            src_ref=rx_ref.at[other, source], dst_ref=rx_ref.at[other, source],
+            send_sem=fsend_sem.at[i], recv_sem=frecv_sem.at[i],
+            device_id=(me, other), device_id_type=MESH,
+        )
+
+    barrier = pltpu.get_barrier_semaphore()
+
+    @pl.loop(0, n - 1)
+    def _(i):
+        pl.semaphore_signal(
+            barrier, inc=1, device_id=(partner(me, n - 1 - i, n), core), device_id_type=MESH
+        )
+
+    pl.semaphore_signal(barrier, inc=1, device_id=(me, other), device_id_type=MESH)
+
+    @pl.loop(0, n)
+    def _(i):
+        load(i).start()
+
+    pl.semaphore_wait(barrier, n)
+
+    @pl.loop(0, n)
+    def _(i):
+        to = partner(me, n - 1 - i, n)
+        load(i).wait()
+        rows = irb_ref[pl.ds(pl.multiple_of(to * al, al), al), :]
+        block = vbuf[i]
+        masked = jnp.where(rows[None] == colx_ref[...], block, jnp.zeros_like(block))
+        low, high = s_ref[0], s_ref[1]
+
+        def pack(first, second):
+            return jnp.dot(
+                first.reshape(half * al, width), low, preferred_element_type=F32
+            ) + jnp.dot(second.reshape(half * al, width), high, preferred_element_type=F32)
+
+        fbuf[...] = pack(masked[:half], masked[half:])
+        pairs = masked.reshape(half, 2, al, width)
+        lcbuf[to] = pack(pairs[:, 0], pairs[:, 1]).astype(BF16).reshape(half, al, 2 * SLOTS)
+        for b in range(al):
+            tx[i, b] = fbuf[pl.ds(b, half, stride=al), :].astype(BF16)
+
+        @pl.when(i < n - 1)
+        def _():
+            send(i).start()
+
+    own = pltpu.make_async_copy(tx.at[n - 1], rx_ref.at[core, me], own_sem)
+    own.start()
+    keep = pltpu.make_async_copy(lcbuf, lc_ref.at[core], lc_sem.at[0])
+    keep.start()
+    give = pltpu.make_async_remote_copy(
+        src_ref=lcbuf, dst_ref=lc_ref.at[core], send_sem=lc_sem.at[1], recv_sem=lc_sem.at[2],
+        device_id=(me, other), device_id_type=MESH,
+    )
+    give.start()
+    own.wait()
+    forward(n - 1).start()
+
+    @pl.loop(0, n - 1)
+    def _(k):
+        i = n - 2 - k
+        arrival(i).wait_recv()
+        forward(i).start()
+
+    @pl.loop(0, n - 1)
+    def _(i):
+        send(i).wait_send()
+
+    @pl.loop(0, n)
+    def _(i):
+        forward(i).wait_send()
+        forwarded(i).wait_recv()
+
+    keep.wait()
+    give.wait_send()
+    pltpu.make_async_remote_copy(
+        src_ref=lcbuf, dst_ref=lc_ref.at[other], send_sem=lc_sem.at[1], recv_sem=lc_sem.at[2],
+        device_id=(me, other), device_id_type=MESH,
+    ).wait_recv()
+
+
+def finish_kernel(
+    lc_ref, rx_ref, w_ref, t_ref, colx_ref, irb_ref, res_ref, pe_ref, vsum_ref, out_ref, ebuf
+):
+    n, half, slots = rx_ref.shape[1], rx_ref.shape[3], rx_ref.shape[4]
+    width = irb_ref.shape[1]
+    num_virt = irb_ref.shape[0]
+    irb = irb_ref[...].reshape(n, 2, half, width)
+    for h in range(2):
+        for core in range(2):
+            mirror = rx_ref[core, :, h].reshape(n * half, slots)
+            span = slice(core * width, (core + 1) * width)
+            for bh in range(2):
+                direct = lc_ref[core, :, 0, bh * half:(bh + 1) * half].reshape(n * half, slots)
+                both = jnp.concatenate([direct, mirror], axis=1)
+                spread = jnp.dot(both, w_ref[core, h, bh], preferred_element_type=F32)
+                spread = spread.astype(BF16).reshape(n, half, width)
+                mask = irb[:, bh] == colx_ref[h, :, span][None]
+                ebuf[:, bh, :, span] = jnp.where(mask, spread, jnp.zeros_like(spread))
+        ladder = lax.dot_general(
+            t_ref[...], ebuf[...].reshape(num_virt, 2 * width),
+            (((1,), (1,)), ((), ())), preferred_element_type=F32,
+        )
+        cols = slice(h * num_virt, (h + 1) * num_virt)
+        total = res_ref[:, cols].astype(F32) + ladder
+        out_ref[:, cols] = (total / (pe_ref[...] - vsum_ref[:, cols])).astype(BF16)
+
+
+def ranks(column_irrep):
+    same = column_irrep[:, None] == column_irrep[None, :]
+    index = jnp.arange(column_irrep.shape[0])
+    return jnp.sum(same & (index[None, :] < index[:, None]), axis=1, dtype=jnp.int32)
+
+
+def local(
+    amplitudes, integrals, virtual_irrep, column_irrep, pair_energy, virtual_energy, residual_in
+):
+    n = lax.axis_size("wide")
+    num_virt, width = virtual_irrep.shape[0], column_irrep.shape[0]
+    al, half = num_virt // n, num_virt // n // 2
+    pairs = pair_energy.shape[0]
+    me, core = lax.axis_index("wide"), lax.axis_index("narrow")
+    first_a = me * al
+    local_irrep = lax.dynamic_slice_in_dim(virtual_irrep, first_a, al, 0)
+
+    amp_all = lax.all_gather(amplitudes, ("wide", "narrow"), axis=0)
+    amp_all = amp_all.reshape(n, 2, amplitudes.shape[0], width)
+    amp_all = lax.dynamic_slice_in_dim(amp_all, core * (n // 2), n // 2, 0)
+    amp = jnp.transpose(amp_all, (0, 2, 1, 3)).reshape(pairs, 2 * width)
+    columns = lax.all_gather(column_irrep, "narrow", axis=0)
+
+    rank = ranks(column_irrep)
+    slot = jnp.arange(2 * SLOTS)
+    shift = jnp.array([0, SLOTS])[:, None, None]
+    inside = (slot >= shift) & (slot < shift + SLOTS)
+    pick = ((rank[None, :, None] + shift == slot) & inside).astype(BF16)
+    colx = (local_irrep[:, None] ^ column_irrep[None, :]).astype(BF16)[:, None, :]
+    irb = jnp.broadcast_to(virtual_irrep.astype(BF16)[:, None], (num_virt, width))
+
+    vmem = pl.BlockSpec(memory_space=pltpu.VMEM)
+    hbm = pl.BlockSpec(memory_space=pl.ANY)
+    lc, rx = pl.pallas_call(
+        functools.partial(exchange_kernel, n),
+        out_shape=(
+            jax.ShapeDtypeStruct((2, n, half, al, 2 * SLOTS), BF16),
+            jax.ShapeDtypeStruct((2, n, al, half, 2 * SLOTS), BF16),
+        ),
+        in_specs=[hbm, vmem, vmem, vmem],
+        out_specs=(hbm, hbm),
+        scratch_shapes=[
+            pltpu.VMEM((n, al, al, width), BF16),
+            pltpu.VMEM((half * al, 2 * SLOTS), F32),
+            pltpu.VMEM((n, al, half, 2 * SLOTS), BF16),
+            pltpu.VMEM((n, half, al, 2 * SLOTS), BF16),
+            pltpu.SemaphoreType.DMA((n,)),
+            pltpu.SemaphoreType.DMA((n,)),
+            pltpu.SemaphoreType.DMA((n,)),
+            pltpu.SemaphoreType.DMA((n,)),
+            pltpu.SemaphoreType.DMA((n,)),
+            pltpu.SemaphoreType.DMA,
+            pltpu.SemaphoreType.DMA((3,)),
+        ],
+        compiler_params=pltpu.CompilerParams(
+            collective_id=0, has_side_effects=True, vmem_limit_bytes=40 * 2**20
+        ),
+        cost_estimate=pl.CostEstimate(
+            flops=4 * al * num_virt * width * 2 * SLOTS,
+            bytes_accessed=200 * 2**20, transcendentals=0,
+        ),
+    )(integrals.reshape(al, num_virt, width), irb, colx, pick)
+
+    rank_all = jax.vmap(ranks)(columns)
+    fits = jnp.max(rank_all) < SLOTS
+    spread = (
+        (rank_all[:, None, None, :] + shift[None] == slot[None, None, :, None])
+        & jnp.swapaxes(inside, 1, 2)[None]
+    )
+    spread = spread.astype(BF16)
+    shape = (2, 2, 2, 2 * SLOTS, width)
+    weights = jnp.concatenate(
+        [jnp.broadcast_to(spread[:, :, None], shape), jnp.broadcast_to(-spread[:, None], shape)],
+        axis=3,
+    )
+    colx_all = (local_irrep[:, None] ^ columns.reshape(1, 2 * width)).astype(BF16)[:, None, :]
+    local_energy = lax.dynamic_slice_in_dim(virtual_energy, first_a, al, 0)
+    vsum = (local_energy[:, None] + virtual_energy[None, :]).reshape(1, al * num_virt)
+
+    def short():
+        whole = lambda *shape: pl.BlockSpec(shape, lambda p: (0,) * len(shape))
+        return pl.pallas_call(
+            finish_kernel,
+            grid=(half,),
+            out_shape=jax.ShapeDtypeStruct(residual_in.shape, BF16),
+            in_specs=[
+                pl.BlockSpec((2, n, 1, al, 2 * SLOTS), lambda p: (0, 0, p, 0, 0)),
+                pl.BlockSpec((2, n, 2, half, 2 * SLOTS), lambda p: (0, 0, p, 0, 0)),
+                whole(2, 2, 2, 4 * SLOTS, width),
+                whole(pairs, 2 * width),
+                pl.BlockSpec((2, 1, 2 * width), lambda p: (p, 0, 0)),
+                whole(num_virt, width),
+                pl.BlockSpec((pairs, 2 * num_virt), lambda p: (0, p)),
+                whole(pairs, 1),
+                pl.BlockSpec((1, 2 * num_virt), lambda p: (0, p)),
+            ],
+            out_specs=pl.BlockSpec((pairs, 2 * num_virt), lambda p: (0, p)),
+            scratch_shapes=[pltpu.VMEM((n, 2, half, 2 * width), BF16)],
+            compiler_params=pltpu.CompilerParams(vmem_limit_bytes=40 * 2**20),
+        )(lc, rx, weights, amp, colx_all, irb, residual_in, pair_energy[:, None], vsum)
+
+    def full():
+        return dense(
+            amplitudes, integrals, virtual_irrep, column_irrep, pair_energy, virtual_energy,
+            residual_in,
+        )
+
+    return lax.cond(fits, short, full)
+
+
 def solution(mesh):
+    usable = mesh.shape["narrow"] == 2 and mesh.shape["wide"] == 16
     return jax.shard_map(
-        local,
+        local if usable else dense,
         mesh=mesh,
         in_specs=(
             P("wide", "narrow"),

time: 359 us -> 143 us (0.40)
  the two profiles are of different devices: /device:TPU:28 before, /device:TPU:0 now
where the time goes in v1:
time: 143 us
  Pallas kernels  80.7 us (56%)
  blocking collectives  41.8 us (29%)
  between operations  14.2 us (10%)
  other arithmetic  4.19 us (3%)
  local copies, waits for them, and re-layouts  1.44 us (1%)
    pallas_call x1, Pallas kernels, local(): pl.pallas_call(functools.partial(exchange_kernel, n), out_shape=(jax.Shap...  61 us
    all_gather x1, blocking collectives, local(): amp_all = lax.all_gather(amplitudes, ('wide', 'narrow'), axis=0)  39.5 us
    pallas_call x1, Pallas kernels, short(): pl.pallas_call(finish_kernel, grid=(half,), out_shape=jax.ShapeDtypeStruc...  19.7 us

profile of v1, /device:TPU:0, one launch (start us, length us, event | category | flops | bytes accessed | tf_op | source)
XLA Modules:
  0.0 142.6 jit_solution(824331257240202850)
XLA Ops:
  6.5 0.0 copy-start.1
  6.5 0.0 copy-start.3
  6.5 0.0 copy-start
  6.5 0.0 copy-start.4
  6.5 0.0 copy-start.2
  6.6 2.3 %all-gather.2 = s32[2,1,256]{2,1,0:T(1,128)S(1)} all-gather(s32[1,1,256]{2,1,0:T(1,128)} %bitcast.52), channel_id=2, replica_groups=mesh['wide'=16,'narrow'=2] {'narrow'}, dimensions={0}, use_global_device_ids=true | all-gather | bytes 3072 | tf_op jit(solution)/shard_map/all_gather | solution.py:232
  8.9 0.2 convert_reduce_fusion
  9.1 0.1 broadcast_add_fusion
  9.2 0.1 compare_and_fusion
  9.2 0.1 fusion.8
  9.4 0.1 fusion.11
  9.6 0.1 pad_maximum_fusion
  9.7 0.8 dynamic_slice.15
  10.4 0.8 xor_convert_fusion.1.colx_ref
  11.2 0.9 convert_reduce_fusion.1
  12.2 0.1 broadcast_add_fusion.1
  12.2 0.1 fusion.10.s_ref
  12.4 0.7 convert_element_type.68
  13.1 0.1 broadcast_in_dim.11.irb_ref
  13.2 61.0 %shard_map.84 = (bf16[2,16,16,32,128]{4,3,2,1,0:T(8,128)(2,1)}, bf16[2,16,32,16,128]{4,3,2,1,0:T(8,128)(2,1)}) custom-call(bf16[32,512,256]{2,1,0:T(8,128)(2,1)} %bitcast.45, bf16[512,256]{1,0:T(8,128)(2,1)S(1)} %broadcast_in_dim.11.irb_ref, bf16[32,1,256]{2,1,0:T(2,128)(2,1)S(1)} %xor_convert_fusion.1.colx_ref, bf16[2,256,128]{2,1,0:T(8,128)(2,1)S(1)} %fusion.10.s_ref), custom_call_target="tpu_custom_call" | custom-call | flops 2147483648 | bytes 209715200 | tf_op jit(solution)/shard_map/pallas_call | solution.py:244
  74.3 0.1 xor_convert_fusion
  74.4 0.0 copy-done
  74.4 39.5 %all-gather.1 = bf16[768,256]{1,0:T(8,128)(2,1)S(1)} all-gather(bf16[24,256]{1,0:T(8,128)(2,1)S(1)} %copy-done), channel_id=3, replica_groups=mesh['wide'=16,'narrow'=2] {'wide','narrow'}, dimensions={0}, use_global_device_ids=true | all-gather | bytes 405504 | tf_op jit(solution)/shard_map/all_gather | solution.py:228
  113.9 0.6 reduce_max.9
  115.2 0.0 copy-done.1
  115.2 0.0 copy-done.3
  115.2 0.0 copy-done.4
  115.2 0.0 copy-done.2
  115.2 20.5 %conditional.1 = (bf16[192,16384]{1,0:T(8,128)(2,1)}) conditional(s32[]{:T(128)} %convert_element_type.67, (bf16[192,16384]{1,0:T(8,128)(2,1)}, s32[512]{0:T(512)S(1)}, s32[256]{0:T(256)S(1)}, bf16[16384,256]{1,0:T(8,128)(2,1)}, bf16[24,256]{1,0:T(8,128)(2,1)S(1)}, /*index=5*/f32[192]{0:T(256)S(1)}, f32[512]{0:T(512)S(1)}) %tuple.42, ...), branch_computations={%region_3.5_spmd, %region_5.6_spmd} | conditional | flops 3257948160 | bytes 227478176 | solution.py:318
  115.5 0.2 copy.41
  115.7 0.1 dynamic_slice.18
  115.8 0.1 add_bitcast_fusion
  115.8 0.1 copy.51
  115.9 0.1 copy.37.pe_ref
  116.0 19.7 %branch_1_fun.1 = bf16[192,16384]{1,0:T(8,128)(2,1)} custom-call(bf16[2,16,16,32,128]{4,3,2,1,0:T(8,128)(2,1)} %get-tuple-element.47.lc_ref, bf16[2,16,32,16,128]{4,3,2,1,0:T(8,128)(2,1)} %get-tuple-element.48.rx_ref, bf16[2,2,2,256,256]{4,3,2,1,0:T(8,128)(2,1)S(1)} %get-tuple-element.49.w_ref, bf16[192,512]{1,0:T(8,128)(2,1)S(1)} %bitcast.42, ...), custom_call_target="tpu_custom_call" | custom-call | tf_op jit(solution)/shard_map/cond/branch_1_fun/pallas_call | solution.py:292
  (7 shorter events, 0.1 us)
Async XLA Ops:
  6.5 108.7 %copy-start.1 = (s32[256]{0:T(256)S(1)}, s32[256]{0:T(256)}, u32[]{:S(2)}) copy-start(s32[256]{0:T(256)} %param.13) | copy-start | bytes 3076
  6.5 108.7 %copy-start.3 = (s32[512]{0:T(512)S(1)}, s32[512]{0:T(512)}, u32[]{:S(2)}) copy-start(s32[512]{0:T(512)} %param.12) | copy-start | bytes 6148
  6.5 67.9 %copy-start = (bf16[24,256]{1,0:T(8,128)(2,1)S(1)}, bf16[24,256]{1,0:T(8,128)(2,1)}, u32[]{:S(2)}) copy-start(bf16[24,256]{1,0:T(8,128)(2,1)} %param.10) | copy-start | bytes 36868
  6.5 108.7 %copy-start.4 = (f32[192]{0:T(256)S(1)}, f32[192]{0:T(256)}, u32[]{:S(2)}) copy-start(f32[192]{0:T(256)} %param.14) | copy-start | bytes 2308
  6.5 108.7 %copy-start.2 = (f32[512]{0:T(512)S(1)}, f32[512]{0:T(512)}, u32[]{:S(2)}) copy-start(f32[512]{0:T(512)} %param.15) | copy-start | bytes 6148

commit v2 on v1

--- a/solution.py
+++ b/solution.py
@@ -62,8 +62,8 @@
 
 
 def exchange_kernel(
-    n, v_ref, irb_ref, colx_ref, s_ref, lc_ref, rx_ref,
-    vbuf, fbuf, tx, lcbuf, load_sem, send_sem, recv_sem, fsend_sem, frecv_sem, own_sem, lc_sem,
+    n, v_ref, irb_ref, colx_ref, s_ref, amp_ref, lc_ref, rx_ref, t_ref,
+    vbuf, fbuf, tx, lcbuf, tbuf, tsend_sem, trecv_sem, tgive_sem, load_sem, send_sem, recv_sem, fsend_sem, frecv_sem, own_sem, lc_sem,
 ):
     me, core = lax.axis_index("wide"), lax.axis_index("narrow")
     other = 1 - core
@@ -106,6 +106,20 @@
             device_id=(me, other), device_id_type=MESH,
         )
 
+    def send_amp(i):
+        return pltpu.make_async_remote_copy(
+            src_ref=amp_ref, dst_ref=tbuf.at[me], send_sem=tsend_sem.at[i],
+            recv_sem=trecv_sem.at[i], device_id=(partner(me, n - 1 - i, n), core),
+            device_id_type=MESH,
+        )
+
+    def arrived_amp(i):
+        source = partner(me, n - 1 - i, n)
+        return pltpu.make_async_remote_copy(
+            src_ref=amp_ref, dst_ref=tbuf.at[source], send_sem=tsend_sem.at[i],
+            recv_sem=trecv_sem.at[i], device_id=(source, core), device_id_type=MESH,
+        )
+
     barrier = pltpu.get_barrier_semaphore()
 
     @pl.loop(0, n - 1)
@@ -120,7 +134,13 @@
     def _(i):
         load(i).start()
 
+    own_amp = pltpu.make_async_copy(amp_ref, tbuf.at[me], own_sem.at[1])
+    own_amp.start()
     pl.semaphore_wait(barrier, n)
+
+    @pl.loop(0, n - 1)
+    def _(i):
+        send_amp(i).start()
 
     @pl.loop(0, n)
     def _(i):
@@ -146,7 +166,7 @@
         def _():
             send(i).start()
 
-    own = pltpu.make_async_copy(tx.at[n - 1], rx_ref.at[core, me], own_sem)
+    own = pltpu.make_async_copy(tx.at[n - 1], rx_ref.at[core, me], own_sem.at[0])
     own.start()
     keep = pltpu.make_async_copy(lcbuf, lc_ref.at[core], lc_sem.at[0])
     keep.start()
@@ -157,6 +177,22 @@
     give.start()
     own.wait()
     forward(n - 1).start()
+    own_amp.wait()
+
+    @pl.loop(0, n - 1)
+    def _(i):
+        arrived_amp(i).wait_recv()
+
+    keep_amp = pltpu.make_async_copy(
+        tbuf.at[pl.ds(core * (n // 2), n // 2)], t_ref.at[core], tgive_sem.at[0]
+    )
+    keep_amp.start()
+    give_amp = pltpu.make_async_remote_copy(
+        src_ref=tbuf.at[pl.ds(other * (n // 2), n // 2)], dst_ref=t_ref.at[core],
+        send_sem=tgive_sem.at[1], recv_sem=tgive_sem.at[2],
+        device_id=(me, other), device_id_type=MESH,
+    )
+    give_amp.start()
 
     @pl.loop(0, n - 1)
     def _(k):
@@ -167,12 +203,20 @@
     @pl.loop(0, n - 1)
     def _(i):
         send(i).wait_send()
+        send_amp(i).wait_send()
 
     @pl.loop(0, n)
     def _(i):
         forward(i).wait_send()
         forwarded(i).wait_recv()
 
+    keep_amp.wait()
+    give_amp.wait_send()
+    pltpu.make_async_remote_copy(
+        src_ref=tbuf.at[pl.ds(other * (n // 2), n // 2)], dst_ref=t_ref.at[other],
+        send_sem=tgive_sem.at[1], recv_sem=tgive_sem.at[2],
+        device_id=(me, other), device_id_type=MESH,
+    ).wait_recv()
     keep.wait()
     give.wait_send()
     pltpu.make_async_remote_copy(
@@ -221,14 +265,10 @@
     num_virt, width = virtual_irrep.shape[0], column_irrep.shape[0]
     al, half = num_virt // n, num_virt // n // 2
     pairs = pair_energy.shape[0]
-    me, core = lax.axis_index("wide"), lax.axis_index("narrow")
+    me = lax.axis_index("wide")
     first_a = me * al
     local_irrep = lax.dynamic_slice_in_dim(virtual_irrep, first_a, al, 0)
 
-    amp_all = lax.all_gather(amplitudes, ("wide", "narrow"), axis=0)
-    amp_all = amp_all.reshape(n, 2, amplitudes.shape[0], width)
-    amp_all = lax.dynamic_slice_in_dim(amp_all, core * (n // 2), n // 2, 0)
-    amp = jnp.transpose(amp_all, (0, 2, 1, 3)).reshape(pairs, 2 * width)
     columns = lax.all_gather(column_irrep, "narrow", axis=0)
 
     rank = ranks(column_irrep)
@@ -241,25 +281,30 @@
 
     vmem = pl.BlockSpec(memory_space=pltpu.VMEM)
     hbm = pl.BlockSpec(memory_space=pl.ANY)
-    lc, rx = pl.pallas_call(
+    lc, rx, amp = pl.pallas_call(
         functools.partial(exchange_kernel, n),
         out_shape=(
             jax.ShapeDtypeStruct((2, n, half, al, 2 * SLOTS), BF16),
             jax.ShapeDtypeStruct((2, n, al, half, 2 * SLOTS), BF16),
+            jax.ShapeDtypeStruct((2, n // 2) + amplitudes.shape, BF16),
         ),
-        in_specs=[hbm, vmem, vmem, vmem],
-        out_specs=(hbm, hbm),
+        in_specs=[hbm, vmem, vmem, vmem, vmem],
+        out_specs=(hbm, hbm, hbm),
         scratch_shapes=[
             pltpu.VMEM((n, al, al, width), BF16),
             pltpu.VMEM((half * al, 2 * SLOTS), F32),
             pltpu.VMEM((n, al, half, 2 * SLOTS), BF16),
             pltpu.VMEM((n, half, al, 2 * SLOTS), BF16),
-            pltpu.SemaphoreType.DMA((n,)),
-            pltpu.SemaphoreType.DMA((n,)),
-            pltpu.SemaphoreType.DMA((n,)),
-            pltpu.SemaphoreType.DMA((n,)),
-            pltpu.SemaphoreType.DMA((n,)),
-            pltpu.SemaphoreType.DMA,
+            pltpu.VMEM((n,) + amplitudes.shape, BF16),
+            pltpu.SemaphoreType.DMA((n,)),
+            pltpu.SemaphoreType.DMA((n,)),
+            pltpu.SemaphoreType.DMA((3,)),
+            pltpu.SemaphoreType.DMA((n,)),
+            pltpu.SemaphoreType.DMA((n,)),
+            pltpu.SemaphoreType.DMA((n,)),
+            pltpu.SemaphoreType.DMA((n,)),
+            pltpu.SemaphoreType.DMA((n,)),
+            pltpu.SemaphoreType.DMA((2,)),
             pltpu.SemaphoreType.DMA((3,)),
         ],
         compiler_params=pltpu.CompilerParams(
@@ -269,7 +314,8 @@
             flops=4 * al * num_virt * width * 2 * SLOTS,
             bytes_accessed=200 * 2**20, transcendentals=0,
         ),
-    )(integrals.reshape(al, num_virt, width), irb, colx, pick)
+    )(integrals.reshape(al, num_virt, width), irb, colx, pick, amplitudes)
+    amp = jnp.transpose(amp.reshape(2, pairs, width), (1, 0, 2)).reshape(pairs, 2 * width)
 
     rank_all = jax.vmap(ranks)(columns)
     fits = jnp.max(rank_all) < SLOTS

time: 143 us -> 111 us (0.78)
  blocking collectives: 41.8 us -> 2.26 us
  Pallas kernels: 80.7 us -> 88.1 us
    all_gather x1 -> x0, blocking collectives: 39.5 us -> none  [local(): amp_all = lax.all_gather(amplitudes, ('wide', 'narrow'), axis=0)]
    pallas_call x1, Pallas kernels: 61 us -> 68.4 us  [local(): pl.pallas_call(functools.partial(exchange_kernel, n), out_shape=(jax.Shap...]
where the time goes in v2:
time: 111 us; the launch traced here: 110 us
  Pallas kernels  88.1 us (79%)
  between operations  14.2 us (13%)
  other arithmetic  4.19 us (4%)
  blocking collectives  2.26 us (2%)
  local copies, waits for them, and re-layouts  1.47 us (1%)
    pallas_call x1, Pallas kernels, local(): pl.pallas_call(functools.partial(exchange_kernel, n), out_shape=(jax.Shap...  68.4 us
    pallas_call x1, Pallas kernels, short(): pl.pallas_call(finish_kernel, grid=(half,), out_shape=jax.ShapeDtypeStruc...  19.7 us
    all_gather x1, blocking collectives, local(): columns = lax.all_gather(column_irrep, 'narrow', axis=0)  2.26 us

profile of v2, /device:TPU:0, one launch (start us, length us, event | category | flops | bytes accessed | tf_op | source)
XLA Modules:
  0.0 110.5 jit_solution(16086511771833554751)
XLA Ops:
  6.5 0.0 copy-start.1
  6.5 0.0 copy-start.3
  6.5 0.0 copy-start
  6.5 0.0 copy-start.4
  6.5 0.0 copy-start.2
  6.6 2.3 %all-gather.1 = s32[2,1,256]{2,1,0:T(1,128)S(1)} all-gather(s32[1,1,256]{2,1,0:T(1,128)} %bitcast.53), channel_id=2, replica_groups=mesh['wide'=16,'narrow'=2] {'narrow'}, dimensions={0}, use_global_device_ids=true | all-gather | bytes 3072 | tf_op jit(solution)/shard_map/all_gather | solution.py:272
  8.9 0.2 convert_reduce_fusion
  9.1 0.1 broadcast_add_fusion
  9.2 0.1 compare_and_fusion
  9.2 0.1 fusion.8
  9.4 0.1 fusion.11
  9.6 0.1 pad_maximum_fusion
  9.7 0.9 convert_reduce_fusion.1
  10.6 0.1 broadcast_add_fusion.1
  10.7 0.1 fusion.10.s_ref
  10.8 0.8 dynamic_slice.12
  11.6 0.8 xor_convert_fusion.1.colx_ref
  12.4 0.7 convert_element_type.68
  13.1 0.1 broadcast_in_dim.11.irb_ref
  13.2 68.4 %shard_map.84 = (bf16[2,16,16,32,128]{4,3,2,1,0:T(8,128)(2,1)}, bf16[2,16,32,16,128]{4,3,2,1,0:T(8,128)(2,1)}, bf16[2,8,24,256]{3,2,1,0:T(8,128)(2,1)S(1)}) custom-call(bf16[32,512,256]{2,1,0:T(8,128)(2,1)} %bitcast.46, bf16[512,256]{1,0:T(8,128)(2,1)S(1)} %broadcast_in_dim.11.irb_ref, bf16[32,1,256]{2,1,0:T(2,128)(2,1)S(1)} %xor_convert_fusion.1.colx_ref, ...), custom_call_target="tpu_custom_call" | custom-call | flops 2147483648 | bytes 209715200 | tf_op jit(solution)/shard_map/pallas_call | solution.py:284
  81.7 0.2 copy.55
  81.9 0.1 xor_convert_fusion
  82.0 0.6 reduce_max.9
  83.3 0.0 copy-done.1
  83.3 0.0 copy-done.3
  83.3 0.0 copy-done
  83.3 0.0 copy-done.4
  83.3 0.0 copy-done.2
  83.3 20.3 %conditional.1 = (bf16[192,16384]{1,0:T(8,128)(2,1)}) conditional(s32[]{:T(128)} %convert_element_type.67, (bf16[192,16384]{1,0:T(8,128)(2,1)}, s32[512]{0:T(512)S(1)}, s32[256]{0:T(256)S(1)}, bf16[16384,256]{1,0:T(8,128)(2,1)}, bf16[24,256]{1,0:T(8,128)(2,1)S(1)}, /*index=5*/f32[192]{0:T(256)S(1)}, f32[512]{0:T(512)S(1)}) %tuple.39, ...), branch_computations={%region_3.5_spmd, %region_5.6_spmd} | conditional | flops 3257948160 | bytes 227478176 | solution.py:364
  83.6 0.1 dynamic_slice.14
  83.7 0.1 add_bitcast_fusion
  83.8 0.1 copy.52
  83.8 0.1 copy.38.pe_ref
  84.0 19.7 %branch_1_fun.1 = bf16[192,16384]{1,0:T(8,128)(2,1)} custom-call(bf16[2,16,16,32,128]{4,3,2,1,0:T(8,128)(2,1)} %get-tuple-element.47.lc_ref, bf16[2,16,32,16,128]{4,3,2,1,0:T(8,128)(2,1)} %get-tuple-element.48.rx_ref, bf16[2,2,2,256,256]{4,3,2,1,0:T(8,128)(2,1)S(1)} %get-tuple-element.49.w_ref, bf16[192,512]{1,0:T(8,128)(2,1)S(1)} %bitcast.42, ...), custom_call_target="tpu_custom_call" | custom-call | tf_op jit(solution)/shard_map/cond/branch_1_fun/pallas_call | solution.py:338
  (6 shorter events, 0.1 us)
Async XLA Ops:
  6.5 76.8 %copy-start.1 = (s32[256]{0:T(256)S(1)}, s32[256]{0:T(256)}, u32[]{:S(2)}) copy-start(s32[256]{0:T(256)} %param.13) | copy-start | bytes 3076
  6.5 76.8 %copy-start.3 = (s32[512]{0:T(512)S(1)}, s32[512]{0:T(512)}, u32[]{:S(2)}) copy-start(s32[512]{0:T(512)} %param.12) | copy-start | bytes 6148
  6.5 76.8 %copy-start = (bf16[24,256]{1,0:T(8,128)(2,1)S(1)}, bf16[24,256]{1,0:T(8,128)(2,1)}, u32[]{:S(2)}) copy-start(bf16[24,256]{1,0:T(8,128)(2,1)} %amp_ref.1) | copy-start | bytes 36868
  6.5 76.8 %copy-start.4 = (f32[192]{0:T(256)S(1)}, f32[192]{0:T(256)}, u32[]{:S(2)}) copy-start(f32[192]{0:T(256)} %param.14) | copy-start | bytes 2308
  6.5 76.8 %copy-start.2 = (f32[512]{0:T(512)S(1)}, f32[512]{0:T(512)}, u32[]{:S(2)}) copy-start(f32[512]{0:T(512)} %param.15) | copy-start | bytes 6148

commit v3 on v2

--- a/solution.py
+++ b/solution.py
@@ -72,26 +72,26 @@
     width = v_ref.shape[2]
 
     def load(i):
-        to = partner(me, n - 1 - i, n)
+        to = partner(me, i + 1, n)
         columns = pl.ds(pl.multiple_of(to * al, al), al)
         return pltpu.make_async_copy(v_ref.at[:, columns, :], vbuf.at[i], load_sem.at[i])
 
     def send(i):
-        to = partner(me, n - 1 - i, n)
+        to = partner(me, i + 1, n)
         return pltpu.make_async_remote_copy(
             src_ref=tx.at[i], dst_ref=rx_ref.at[core, me], send_sem=send_sem.at[i],
             recv_sem=recv_sem.at[i], device_id=(to, core), device_id_type=MESH,
         )
 
     def arrival(i):
-        source = partner(me, n - 1 - i, n)
+        source = partner(me, i + 1, n)
         return pltpu.make_async_remote_copy(
             src_ref=tx.at[i], dst_ref=rx_ref.at[core, source], send_sem=send_sem.at[i],
             recv_sem=recv_sem.at[i], device_id=(source, core), device_id_type=MESH,
         )
 
     def forward(i):
-        source = partner(me, n - 1 - i, n)
+        source = partner(me, i + 1, n)
         return pltpu.make_async_remote_copy(
             src_ref=rx_ref.at[core, source], dst_ref=rx_ref.at[core, source],
             send_sem=fsend_sem.at[i], recv_sem=frecv_sem.at[i],
@@ -99,7 +99,7 @@
         )
 
     def forwarded(i):
-        source = partner(me, n - 1 - i, n)
+        source = partner(me, i + 1, n)
         return pltpu.make_async_remote_copy(
             src_ref=rx_ref.at[other, source], dst_ref=rx_ref.at[other, source],
             send_sem=fsend_sem.at[i], recv_sem=frecv_sem.at[i],
@@ -109,12 +109,12 @@
     def send_amp(i):
         return pltpu.make_async_remote_copy(
             src_ref=amp_ref, dst_ref=tbuf.at[me], send_sem=tsend_sem.at[i],
-            recv_sem=trecv_sem.at[i], device_id=(partner(me, n - 1 - i, n), core),
+            recv_sem=trecv_sem.at[i], device_id=(partner(me, i + 1, n), core),
             device_id_type=MESH,
         )
 
     def arrived_amp(i):
-        source = partner(me, n - 1 - i, n)
+        source = partner(me, i + 1, n)
         return pltpu.make_async_remote_copy(
             src_ref=amp_ref, dst_ref=tbuf.at[source], send_sem=tsend_sem.at[i],
             recv_sem=trecv_sem.at[i], device_id=(source, core), device_id_type=MESH,
@@ -125,7 +125,7 @@
     @pl.loop(0, n - 1)
     def _(i):
         pl.semaphore_signal(
-            barrier, inc=1, device_id=(partner(me, n - 1 - i, n), core), device_id_type=MESH
+            barrier, inc=1, device_id=(partner(me, i + 1, n), core), device_id_type=MESH
         )
 
     pl.semaphore_signal(barrier, inc=1, device_id=(me, other), device_id_type=MESH)
@@ -144,7 +144,7 @@
 
     @pl.loop(0, n)
     def _(i):
-        to = partner(me, n - 1 - i, n)
+        to = partner(me, i + 1, n)
         load(i).wait()
         rows = irb_ref[pl.ds(pl.multiple_of(to * al, al), al), :]
         block = vbuf[i]
@@ -195,8 +195,7 @@
     give_amp.start()
 
     @pl.loop(0, n - 1)
-    def _(k):
-        i = n - 2 - k
+    def _(i):
         arrival(i).wait_recv()
         forward(i).start()
 

time: 111 us -> 102 us (0.919)
  the two profiles are of different devices: /device:TPU:0 before, /device:TPU:9 now
where the time goes in v3:
time: 102 us; the launch traced here: 101 us
  Pallas kernels  78.7 us (77%)
  between operations  14.2 us (14%)
  other arithmetic  4.19 us (4%)
  blocking collectives  2.48 us (2%)
  local copies, waits for them, and re-layouts  1.47 us (1%)
    pallas_call x1, Pallas kernels, local(): pl.pallas_call(functools.partial(exchange_kernel, n), out_shape=(jax.Shap...  59 us
    pallas_call x1, Pallas kernels, short(): pl.pallas_call(finish_kernel, grid=(half,), out_shape=jax.ShapeDtypeStruc...  19.7 us
    all_gather x1, blocking collectives, local(): columns = lax.all_gather(column_irrep, 'narrow', axis=0)  2.48 us

profile of v3, /device:TPU:9, one launch (start us, length us, event | category | flops | bytes accessed | tf_op | source)
XLA Modules:
  0.0 101.2 jit_solution(5244389820078035037)
XLA Ops:
  6.5 0.0 copy-start.1
  6.5 0.0 copy-start.3
  6.5 0.0 copy-start
  6.5 0.0 copy-start.4
  6.5 0.0 copy-start.2
  6.6 2.5 %all-gather.1 = s32[2,1,256]{2,1,0:T(1,128)S(1)} all-gather(s32[1,1,256]{2,1,0:T(1,128)} %bitcast.53), channel_id=2, replica_groups=mesh['wide'=16,'narrow'=2] {'narrow'}, dimensions={0}, use_global_device_ids=true | all-gather | bytes 3072 | tf_op jit(solution)/shard_map/all_gather | solution.py:271
  9.1 0.2 convert_reduce_fusion
  9.3 0.1 broadcast_add_fusion
  9.4 0.1 compare_and_fusion
  9.5 0.1 fusion.8
  9.6 0.1 fusion.11
  9.8 0.1 pad_maximum_fusion
  9.9 0.9 convert_reduce_fusion.1
  10.8 0.1 broadcast_add_fusion.1
  10.9 0.1 fusion.10.s_ref
  11.1 0.8 dynamic_slice.12
  11.8 0.8 xor_convert_fusion.1.colx_ref
  12.6 0.7 convert_element_type.68
  13.3 0.1 broadcast_in_dim.11.irb_ref
  13.4 59.0 %shard_map.84 = (bf16[2,16,16,32,128]{4,3,2,1,0:T(8,128)(2,1)}, bf16[2,16,32,16,128]{4,3,2,1,0:T(8,128)(2,1)}, bf16[2,8,24,256]{3,2,1,0:T(8,128)(2,1)S(1)}) custom-call(bf16[32,512,256]{2,1,0:T(8,128)(2,1)} %bitcast.46, bf16[512,256]{1,0:T(8,128)(2,1)S(1)} %broadcast_in_dim.11.irb_ref, bf16[32,1,256]{2,1,0:T(2,128)(2,1)S(1)} %xor_convert_fusion.1.colx_ref, ...), custom_call_target="tpu_custom_call" | custom-call | flops 2147483648 | bytes 209715200 | tf_op jit(solution)/shard_map/pallas_call | solution.py:283
  72.4 0.2 copy.55
  72.6 0.1 xor_convert_fusion
  72.8 0.6 reduce_max.9
  74.1 0.0 copy-done.1
  74.1 0.0 copy-done.3
  74.1 0.0 copy-done
  74.1 0.0 copy-done.4
  74.1 0.0 copy-done.2
  74.1 20.3 %conditional.1 = (bf16[192,16384]{1,0:T(8,128)(2,1)}) conditional(s32[]{:T(128)} %convert_element_type.67, (bf16[192,16384]{1,0:T(8,128)(2,1)}, s32[512]{0:T(512)S(1)}, s32[256]{0:T(256)S(1)}, bf16[16384,256]{1,0:T(8,128)(2,1)}, bf16[24,256]{1,0:T(8,128)(2,1)S(1)}, /*index=5*/f32[192]{0:T(256)S(1)}, f32[512]{0:T(512)S(1)}) %tuple.39, ...), branch_computations={%region_3.5_spmd, %region_5.6_spmd} | conditional | flops 3257948160 | bytes 227478176 | solution.py:363
  74.4 0.1 dynamic_slice.14
  74.5 0.1 add_bitcast_fusion
  74.5 0.1 copy.52
  74.6 0.1 copy.38.pe_ref
  74.7 19.7 %branch_1_fun.1 = bf16[192,16384]{1,0:T(8,128)(2,1)} custom-call(bf16[2,16,16,32,128]{4,3,2,1,0:T(8,128)(2,1)} %get-tuple-element.47.lc_ref, bf16[2,16,32,16,128]{4,3,2,1,0:T(8,128)(2,1)} %get-tuple-element.48.rx_ref, bf16[2,2,2,256,256]{4,3,2,1,0:T(8,128)(2,1)S(1)} %get-tuple-element.49.w_ref, bf16[192,512]{1,0:T(8,128)(2,1)S(1)} %bitcast.42, ...), custom_call_target="tpu_custom_call" | custom-call | tf_op jit(solution)/shard_map/cond/branch_1_fun/pallas_call | solution.py:337
  (6 shorter events, 0.1 us)
Async XLA Ops:
  6.5 67.5 %copy-start.1 = (s32[256]{0:T(256)S(1)}, s32[256]{0:T(256)}, u32[]{:S(2)}) copy-start(s32[256]{0:T(256)} %param.13) | copy-start | bytes 3076
  6.5 67.5 %copy-start.3 = (s32[512]{0:T(512)S(1)}, s32[512]{0:T(512)}, u32[]{:S(2)}) copy-start(s32[512]{0:T(512)} %param.12) | copy-start | bytes 6148
  6.5 67.5 %copy-start = (bf16[24,256]{1,0:T(8,128)(2,1)S(1)}, bf16[24,256]{1,0:T(8,128)(2,1)}, u32[]{:S(2)}) copy-start(bf16[24,256]{1,0:T(8,128)(2,1)} %amp_ref.1) | copy-start | bytes 36868
  6.5 67.5 %copy-start.4 = (f32[192]{0:T(256)S(1)}, f32[192]{0:T(256)}, u32[]{:S(2)}) copy-start(f32[192]{0:T(256)} %param.14) | copy-start | bytes 2308
  6.5 67.6 %copy-start.2 = (f32[512]{0:T(512)S(1)}, f32[512]{0:T(512)}, u32[]{:S(2)}) copy-start(f32[512]{0:T(512)} %param.15) | copy-start | bytes 6148
